TPU v7x, 32 devices: a whole 2x2x4 slice. The times are simulated.
32 devices in a mesh: layer: 4 (over y, x), feat: 8 (over z, core).
Axes of the slice: x: 2, y: 2, z: 4, core: 2. Of those that a mesh axis runs over, the one named last changes fastest.
Arguments:
- source_decoder: bfloat16 [4, 1024, 8192], P('layer', 'feat'), may hold values from -0.0625 to 0.0625
- reader_encoder: bfloat16 [4, 8192, 6144], P('layer', None, 'feat'), may hold values from -6 to 6
- source_acts: bfloat16 [2048, 4096], P('feat', 'layer'), may hold values from 0 to 2
- target_grads: bfloat16 [2048, 24576], P('feat', 'layer'), may hold values from -0.13183594 to 0.13183594
- pair_source: int32 [4, 8, 24], P('layer', 'feat'), may hold values from 0 to 3
- pair_target: int32 [4, 8, 24], P('layer', 'feat'), may hold values from 0 to 5
- pair_count: int32 [4, 8], P('layer', 'feat'), may hold values from 1 to 24, as said below
Outputs:
- edge_table: float32 [4, 8, 24, 128, 128], P('layer', 'feat')
Inputs may be any that keep to these rules, and one draw needn't show every extreme that they name: `pair_count`: slots at and past the count of a reader layer and column are unused; in every draw some reader layer and column uses all 24 slots.
All inputs are finite; a program needn't handle non-finite values.
Results may differ from a plain program's by a relative error of at most 0.0003.
Values may be sent and summed in bfloat16 or wider, within the bound.
A program may use at most 192 MiB of HBM per device.

v0:
```python
import functools

import jax
import jax.numpy as jnp
from jax import lax
from jax.experimental import pallas as pl
from jax.experimental.pallas import tpu as pltpu
from jax.sharding import PartitionSpec as P

MESH = pl.DeviceIdType.MESH
K_TILE = 1024


def kernel(
    layers,
    feats,
    dec_hbm,
    enc_hbm,
    act_hbm,
    grad_hbm,
    src_ref,
    tgt_ref,
    count_ref,
    out_ref,
    dec,
    enc,
    act,
    grad,
    virt,
    coact,
    edges,
    dec_send,
    dec_recv,
    ring_send,
    ring_recv,
    act_send,
    act_recv,
    grad_send,
    grad_recv,
    local_sem,
):
    me_l = lax.axis_index("layer")
    me_f = lax.axis_index("feat")
    blk, width = dec.shape[1], dec.shape[2]
    tokens = grad.shape[1]
    cols = grad.shape[2]
    targets = cols // blk
    half = width // 2
    half_f = feats // 2
    square = layers == 4

    def peer(j):
        if square:
            y, x = me_l // 2, me_l % 2
            y = 1 - y if j & 2 else y
            x = 1 - x if j & 1 else x
            return y * 2 + x
        return (me_l + j) % layers

    def origin(j):
        return peer(j) if square else (me_l + layers - j) % layers

    direct = (1, 2) if square else tuple(range(1, layers))

    barrier = pltpu.get_barrier_semaphore()
    for j in range(1, layers):
        pl.semaphore_signal(barrier, inc=1, device_id=(peer(j), me_f), device_id_type=MESH)
    for i in range(1, feats):
        pl.semaphore_signal(
            barrier, inc=1, device_id=(me_l, (me_f + i) % feats), device_id_type=MESH
        )

    dec_own = pltpu.make_async_copy(dec_hbm.at[0], dec.at[0], local_sem.at[0])
    enc_own = pltpu.make_async_copy(enc_hbm.at[0], enc, local_sem.at[1])
    my_act = pl.ds(pl.multiple_of(me_f * blk, blk), blk)
    act_own = pltpu.make_async_copy(act_hbm.at[:, my_act], act.at[0, me_f], local_sem.at[2])
    my_grad = pl.ds(pl.multiple_of(me_f * cols, cols), cols)
    grad_own = pltpu.make_async_copy(grad_hbm.at[:, my_grad], grad.at[me_f], local_sem.at[3])

    def act_a2a(i):
        to = (me_f + i) % feats
        return pltpu.make_async_remote_copy(
            src_ref=act_hbm.at[:, pl.ds(pl.multiple_of(to * blk, blk), blk)],
            dst_ref=act.at[0, me_f],
            send_sem=act_send.at[i],
            recv_sem=act_recv.at[i],
            device_id=(me_l, to),
            device_id_type=MESH,
        )

    def grad_a2a(i):
        to = (me_f + i) % feats
        return pltpu.make_async_remote_copy(
            src_ref=grad_hbm.at[:, pl.ds(pl.multiple_of(to * cols, cols), cols)],
            dst_ref=grad.at[me_f],
            send_sem=grad_send.at[i],
            recv_sem=grad_recv.at[i],
            device_id=(me_l, to),
            device_id_type=MESH,
        )

    def dec_copy(j, h, via=None):
        columns = pl.ds(h * half, half)
        hop = j if via is None else j ^ via
        src = dec_hbm.at[0, :, columns] if via is None else dec.at[via, :, columns]
        return pltpu.make_async_remote_copy(
            src_ref=src,
            dst_ref=dec.at[j, :, columns],
            send_sem=dec_send.at[j, h],
            recv_sem=dec_recv.at[j, h],
            device_id=(peer(hop), me_f),
            device_id_type=MESH,
        )

    def act_copy(j, h, via=0):
        rows = pl.ds(h * half_f, half_f)
        return pltpu.make_async_remote_copy(
            src_ref=act.at[via, rows],
            dst_ref=act.at[j, rows],
            send_sem=ring_send.at[j, h],
            recv_sem=ring_recv.at[j, h],
            device_id=(peer(j ^ via), me_f),
            device_id_type=MESH,
        )

    enc_own.start()
    dec_own.start()
    act_own.start()
    grad_own.start()
    pl.semaphore_wait(barrier, layers + feats - 2)

    act_moves = [act_a2a(i) for i in range(1, feats)]
    grad_moves = [grad_a2a(i) for i in range(1, feats)]
    dec_moves = {}
    ring_moves = {}
    for move in act_moves:
        move.start()
    for step in (0, 1):
        for j in direct:
            h = step if j == 2 else 1 - step
            dec_moves[j, h] = dec_copy(j, h)
            dec_moves[j, h].start()
    for move in grad_moves:
        move.start()

    def multiply(j, h):
        @pl.loop(0, half // K_TILE)
        def _(step):
            depth = pl.ds(pl.multiple_of(h * half + step * K_TILE, K_TILE), K_TILE)
            virt[j] += jnp.dot(dec[j, :, depth], enc[depth, :], preferred_element_type=jnp.float32)

    def correlate(f):
        @pl.loop(0, layers)
        def _(j):
            coact[j] += lax.dot_general(
                act[j, f], grad[f], (((0,), (0,)), ((), ())), preferred_element_type=jnp.float32
            )

    virt[...] = jnp.zeros_like(virt)
    coact[...] = jnp.zeros_like(coact)

    act_own.wait()
    for move in act_moves:
        move.wait_recv()
    for h in (0, 1):
        for j in direct:
            ring_moves[j, h] = act_copy(j, h)
            ring_moves[j, h].start()

    enc_own.wait()
    dec_own.wait()
    multiply(0, 0)
    multiply(0, 1)

    if square:
        for via, h in ((1, 1), (2, 0)):
            dec_moves[via, h].wait_recv()
            dec_moves[3, h] = dec_copy(3, h, via)
            dec_moves[3, h].start()
        multiply(1, 1)
        multiply(2, 0)
        for via, h in ((1, 1), (2, 0)):
            ring_moves[via, h].wait_recv()
            ring_moves[3, h] = act_copy(3, h, via)
            ring_moves[3, h].start()
        for j, h in ((1, 0), (2, 1)):
            dec_moves[j, h].wait_recv()
            multiply(j, h)
        for j, h in ((1, 0), (2, 1), (3, 0), (3, 1)):
            ring_moves[j, h].wait_recv()
    else:
        for j in direct:
            for h in (0, 1):
                dec_moves[j, h].wait_recv()
                multiply(j, h)
        for j in direct:
            for h in (0, 1):
                ring_moves[j, h].wait_recv()

    grad_own.wait()
    correlate(me_f)
    for i in range(1, feats):
        grad_moves[i - 1].wait_recv()
        correlate((me_f + feats - i) % feats)
    if square:
        for h in (0, 1):
            dec_moves[3, h].wait_recv()
            multiply(3, h)

    for j in range(layers):
        base = origin(j) * targets if j else me_l * targets
        for t in range(targets):
            block = pl.ds(t * blk, blk)
            edges[base + t] = virt[j, :, block] * coact[j, :, block]

    live = count_ref[0, 0]

    @pl.loop(0, out_ref.shape[2])
    def _(p):
        pair = src_ref[0, 0, p] * targets + tgt_ref[0, 0, p]
        edge = edges[pair]
        out_ref[0, 0, p] = jnp.where(p < live, edge, jnp.zeros_like(edge))

    for move in act_moves + grad_moves + list(dec_moves.values()) + list(ring_moves.values()):
        move.wait_send()


def solution(mesh):
    layers, feats = mesh.shape["layer"], mesh.shape["feat"]
    in_specs = (
        P("layer", "feat", None),
        P("layer", None, "feat"),
        P("feat", "layer"),
        P("feat", "layer"),
        P("layer", "feat", None),
        P("layer", "feat", None),
        P("layer", "feat"),
    )
    out_specs = P("layer", "feat", None, None, None)

    def local(dec, enc, act, grad, src, tgt, count):
        blk, width = dec.shape[1], dec.shape[2]
        cols = enc.shape[2]
        tokens = act.shape[0]
        slots = src.shape[2]
        smem = pl.BlockSpec(memory_space=pltpu.SMEM)
        hbm = pl.BlockSpec(memory_space=pl.ANY)
        dma = pltpu.SemaphoreType.DMA
        return pl.pallas_call(
            functools.partial(kernel, layers, feats),
            out_shape=jax.ShapeDtypeStruct((1, 1, slots, blk, blk), jnp.float32),
            in_specs=[hbm] * 4 + [smem] * 3,
            out_specs=pl.BlockSpec(memory_space=pltpu.VMEM),
            scratch_shapes=[
                pltpu.VMEM((layers, blk, width), dec.dtype),
                pltpu.VMEM((width, cols), enc.dtype),
                pltpu.VMEM((layers, feats, tokens, blk), act.dtype),
                pltpu.VMEM((feats, tokens, cols), grad.dtype),
                pltpu.VMEM((layers, blk, cols), jnp.float32),
                pltpu.VMEM((layers, blk, cols), jnp.float32),
                pltpu.VMEM((layers * (cols // blk), blk, blk), jnp.float32),
                dma((layers, 2)),
                dma((layers, 2)),
                dma((layers, 2)),
                dma((layers, 2)),
                dma((feats,)),
                dma((feats,)),
                dma((feats,)),
                dma((feats,)),
                dma((4,)),
            ],
            compiler_params=pltpu.CompilerParams(
                collective_id=0, has_side_effects=True, vmem_limit_bytes=62 * 1024 * 1024
            ),
            cost_estimate=pl.CostEstimate(
                flops=2 * layers * blk * cols * (width + tokens * feats),
                bytes_accessed=2 * (width * (cols + blk) + tokens * feats * (cols + blk)),
                transcendentals=0,
            ),
        )(dec, enc, act, grad, src, tgt, count)

    return jax.shard_map(local, mesh=mesh, in_specs=in_specs, out_specs=out_specs, check_vma=False)
```

profile of v0, /device:TPU:0, one launch (start us, length us, event | category | flops | bytes accessed | tf_op | source)
XLA Modules:
  0.0 109.2 jit_solution(13654813005186415079)
XLA Ops:
  0.7 105.8 %shard_map.73 = f32[1,1,24,128,128]{4,3,2,1,0:T(8,128)} custom-call(bf16[1,128,8192]{2,1,0:T(8,128)(2,1)} %dec_hbm.1, bf16[1,8192,768]{2,1,0:T(8,128)(2,1)} %enc_hbm.1, bf16[256,1024]{1,0:T(8,128)(2,1)} %act_hbm.1, bf16[256,6144]{1,0:T(8,128)(2,1)} %grad_hbm.1, s32[1,1,24]{2,1,0:T(1,128)} %src_ref.1, s32[1,1,24]{2,1,0:T(1,128)} %tgt_ref.1, ...), custom_call_target="tpu_custom_call" | custom-call | flops 8053063680 | bytes 18350080 | tf_op jit(solution)/shard_map/pallas_call | solution.py:249
  106.5 2.7 %copy.10 = f32[1,1,24,128,128]{4,3,2,1,0:T(8,128)} copy(f32[1,1,24,128,128]{4,3,2,1,0:T(8,128)} %shard_map.73) | data formatting | bytes 3145728
where the time goes:
time: 109 us
  Pallas kernels  106 us (97%)
  local copies, waits for them, and re-layouts  2.7 us (2%)
    pallas_call x1, Pallas kernels, local(): pl.pallas_call(functools.partial(kernel, layers, feats), out_shape=jax.Sh...  106 us
    unnamed x1, local copies, waits for them, and re-layouts  2.7 us

commit v1 on v0

--- a/solution.py
+++ b/solution.py
@@ -20,7 +20,6 @@
     grad_hbm,
     src_ref,
     tgt_ref,
-    count_ref,
     out_ref,
     dec,
     enc,
@@ -45,9 +44,10 @@
     tokens = grad.shape[1]
     cols = grad.shape[2]
     targets = cols // blk
-    half = width // 2
+    square = layers == 4
+    parts = 2
+    piece = width // parts
     half_f = feats // 2
-    square = layers == 4
 
     def peer(j):
         if square:
@@ -73,7 +73,7 @@
     dec_own = pltpu.make_async_copy(dec_hbm.at[0], dec.at[0], local_sem.at[0])
     enc_own = pltpu.make_async_copy(enc_hbm.at[0], enc, local_sem.at[1])
     my_act = pl.ds(pl.multiple_of(me_f * blk, blk), blk)
-    act_own = pltpu.make_async_copy(act_hbm.at[:, my_act], act.at[0, me_f], local_sem.at[2])
+    act_own = pltpu.make_async_copy(act_hbm.at[:, my_act], act.at[me_f, :, pl.ds(0, blk)], local_sem.at[2])
     my_grad = pl.ds(pl.multiple_of(me_f * cols, cols), cols)
     grad_own = pltpu.make_async_copy(grad_hbm.at[:, my_grad], grad.at[me_f], local_sem.at[3])
 
@@ -81,7 +81,7 @@
         to = (me_f + i) % feats
         return pltpu.make_async_remote_copy(
             src_ref=act_hbm.at[:, pl.ds(pl.multiple_of(to * blk, blk), blk)],
-            dst_ref=act.at[0, me_f],
+            dst_ref=act.at[me_f, :, pl.ds(0, blk)],
             send_sem=act_send.at[i],
             recv_sem=act_recv.at[i],
             device_id=(me_l, to),
@@ -100,7 +100,7 @@
         )
 
     def dec_copy(j, h, via=None):
-        columns = pl.ds(h * half, half)
+        columns = pl.ds(h * piece, piece)
         hop = j if via is None else j ^ via
         src = dec_hbm.at[0, :, columns] if via is None else dec.at[via, :, columns]
         return pltpu.make_async_remote_copy(
@@ -115,8 +115,8 @@
     def act_copy(j, h, via=0):
         rows = pl.ds(h * half_f, half_f)
         return pltpu.make_async_remote_copy(
-            src_ref=act.at[via, rows],
-            dst_ref=act.at[j, rows],
+            src_ref=act.at[rows, :, pl.ds(via * blk, blk)],
+            dst_ref=act.at[rows, :, pl.ds(j * blk, blk)],
             send_sem=ring_send.at[j, h],
             recv_sem=ring_recv.at[j, h],
             device_id=(peer(j ^ via), me_f),
@@ -135,91 +135,101 @@
     ring_moves = {}
     for move in act_moves:
         move.start()
-    for step in (0, 1):
+    turns = {1: (1, 0), 2: (0, 1)}
+
+    def send_own(step):
         for j in direct:
-            h = step if j == 2 else 1 - step
+            h = turns[j][step] if square else step
             dec_moves[j, h] = dec_copy(j, h)
             dec_moves[j, h].start()
+
+    for step in range(parts):
+        send_own(step)
     for move in grad_moves:
         move.start()
 
     def multiply(j, h):
-        @pl.loop(0, half // K_TILE)
+        @pl.loop(0, piece // K_TILE)
         def _(step):
-            depth = pl.ds(pl.multiple_of(h * half + step * K_TILE, K_TILE), K_TILE)
+            depth = pl.ds(pl.multiple_of(h * piece + step * K_TILE, K_TILE), K_TILE)
             virt[j] += jnp.dot(dec[j, :, depth], enc[depth, :], preferred_element_type=jnp.float32)
 
     def correlate(f):
-        @pl.loop(0, layers)
-        def _(j):
-            coact[j] += lax.dot_general(
-                act[j, f], grad[f], (((0,), (0,)), ((), ())), preferred_element_type=jnp.float32
-            )
+        coact[...] += lax.dot_general(
+            act[f], grad[f], (((0,), (0,)), ((), ())), preferred_element_type=jnp.float32
+        )
+
+    def receive(j, h):
+        dec_moves[j, h].wait_recv()
+        multiply(j, h)
+
+    def receive_grad(i):
+        grad_moves[i - 1].wait_recv()
+        correlate((me_f + feats - i) % feats)
+
+    arrivals = [i for k in range(1, feats // 2) for i in (k, feats - k)] + [feats // 2]
 
     virt[...] = jnp.zeros_like(virt)
     coact[...] = jnp.zeros_like(coact)
-
     act_own.wait()
     for move in act_moves:
         move.wait_recv()
     for h in (0, 1):
         for j in direct:
-            ring_moves[j, h] = act_copy(j, h)
-            ring_moves[j, h].start()
+            part = 1 - h if j == 1 else h
+            ring_moves[j, part] = act_copy(j, part)
+            ring_moves[j, part].start()
 
     enc_own.wait()
     dec_own.wait()
-    multiply(0, 0)
-    multiply(0, 1)
+    for h in range(parts):
+        multiply(0, h)
+
 
     if square:
-        for via, h in ((1, 1), (2, 0)):
-            dec_moves[via, h].wait_recv()
-            dec_moves[3, h] = dec_copy(3, h, via)
-            dec_moves[3, h].start()
-        multiply(1, 1)
-        multiply(2, 0)
         for via, h in ((1, 1), (2, 0)):
             ring_moves[via, h].wait_recv()
             ring_moves[3, h] = act_copy(3, h, via)
             ring_moves[3, h].start()
-        for j, h in ((1, 0), (2, 1)):
-            dec_moves[j, h].wait_recv()
-            multiply(j, h)
-        for j, h in ((1, 0), (2, 1), (3, 0), (3, 1)):
-            ring_moves[j, h].wait_recv()
+        for step in (0,):
+            ready = ((1, turns[1][step]), (2, turns[2][step]))
+            for via, h in ready:
+                dec_moves[via, h].wait_recv()
+                dec_moves[3, h] = dec_copy(3, h, via)
+                dec_moves[3, h].start()
+            for key in ready:
+                multiply(*key)
+        for key in ((1, 0), (2, 1)):
+            receive(*key)
+        for key in ((1, 0), (2, 1), (3, 0), (3, 1)):
+            ring_moves[key].wait_recv()
+        last = ((3, 0), (3, 1))
     else:
         for j in direct:
             for h in (0, 1):
-                dec_moves[j, h].wait_recv()
-                multiply(j, h)
-        for j in direct:
-            for h in (0, 1):
                 ring_moves[j, h].wait_recv()
+        last = tuple((j, h) for j in direct for h in (0, 1))
 
     grad_own.wait()
     correlate(me_f)
-    for i in range(1, feats):
-        grad_moves[i - 1].wait_recv()
-        correlate((me_f + feats - i) % feats)
-    if square:
-        for h in (0, 1):
-            dec_moves[3, h].wait_recv()
-            multiply(3, h)
+    for i in arrivals[:4]:
+        receive_grad(i)
+    for key in last[:2]:
+        receive(*key)
+    for i in arrivals[4:]:
+        receive_grad(i)
+    for key in last[2:]:
+        receive(*key)
 
     for j in range(layers):
         base = origin(j) * targets if j else me_l * targets
         for t in range(targets):
             block = pl.ds(t * blk, blk)
-            edges[base + t] = virt[j, :, block] * coact[j, :, block]
-
-    live = count_ref[0, 0]
+            edges[base + t] = virt[j, :, block] * coact[pl.ds(j * blk, blk), block]
 
     @pl.loop(0, out_ref.shape[2])
     def _(p):
-        pair = src_ref[0, 0, p] * targets + tgt_ref[0, 0, p]
-        edge = edges[pair]
-        out_ref[0, 0, p] = jnp.where(p < live, edge, jnp.zeros_like(edge))
+        out_ref[0, 0, p] = edges[src_ref[0, 0, p] * targets + tgt_ref[0, 0, p]]
 
     for move in act_moves + grad_moves + list(dec_moves.values()) + list(ring_moves.values()):
         move.wait_send()
@@ -246,21 +256,21 @@
         smem = pl.BlockSpec(memory_space=pltpu.SMEM)
         hbm = pl.BlockSpec(memory_space=pl.ANY)
         dma = pltpu.SemaphoreType.DMA
-        return pl.pallas_call(
+        edges = pl.pallas_call(
             functools.partial(kernel, layers, feats),
             out_shape=jax.ShapeDtypeStruct((1, 1, slots, blk, blk), jnp.float32),
-            in_specs=[hbm] * 4 + [smem] * 3,
+            in_specs=[hbm] * 4 + [smem] * 2,
             out_specs=pl.BlockSpec(memory_space=pltpu.VMEM),
             scratch_shapes=[
                 pltpu.VMEM((layers, blk, width), dec.dtype),
                 pltpu.VMEM((width, cols), enc.dtype),
-                pltpu.VMEM((layers, feats, tokens, blk), act.dtype),
+                pltpu.VMEM((feats, tokens, layers * blk), act.dtype),
                 pltpu.VMEM((feats, tokens, cols), grad.dtype),
                 pltpu.VMEM((layers, blk, cols), jnp.float32),
-                pltpu.VMEM((layers, blk, cols), jnp.float32),
+                pltpu.VMEM((layers * blk, cols), jnp.float32),
                 pltpu.VMEM((layers * (cols // blk), blk, blk), jnp.float32),
-                dma((layers, 2)),
-                dma((layers, 2)),
+                dma((layers, 4)),
+                dma((layers, 4)),
                 dma((layers, 2)),
                 dma((layers, 2)),
                 dma((feats,)),
@@ -277,6 +287,8 @@
                 bytes_accessed=2 * (width * (cols + blk) + tokens * feats * (cols + blk)),
                 transcendentals=0,
             ),
-        )(dec, enc, act, grad, src, tgt, count)
+        )(dec, enc, act, grad, src, tgt)
+        live = jnp.arange(slots)[None, None, :, None, None] < count[:, :, None, None, None]
+        return jnp.where(live, edges, 0.0)
 
     return jax.shard_map(local, mesh=mesh, in_specs=in_specs, out_specs=out_specs, check_vma=False)

time: 109 us -> 103 us (0.945)
  Pallas kernels: 106 us -> 99.4 us
  other arithmetic: 0 us -> 2.73 us
  local copies, waits for them, and re-layouts: 2.7 us -> 0 us
    pallas_call x1, Pallas kernels: 106 us -> 99.4 us  [local(): pl.pallas_call(functools.partial(kernel, layers, feats), out_shape=jax.Sh...]
    select_n x0 -> x1, other arithmetic: none -> 2.72 us  [local(): return jnp.where(live, edges, 0.0)]
    unnamed x1 -> x0, local copies, waits for them, and re-layouts: 2.7 us -> none
where the time goes in v1:
time: 103 us
  Pallas kernels  99.4 us (97%)
  other arithmetic  2.73 us (3%)
    pallas_call x1, Pallas kernels, local(): pl.pallas_call(functools.partial(kernel, layers, feats), out_shape=jax.Sh...  99.4 us
    select_n x1, other arithmetic, local(): return jnp.where(live, edges, 0.0)  2.72 us

profile of v1, /device:TPU:0, one launch (start us, length us, event | category | flops | bytes accessed | tf_op | source)
XLA Modules:
  0.0 102.8 jit_solution(14015644691753314892)
XLA Ops:
  0.7 99.4 %shard_map.73 = f32[1,1,24,128,128]{4,3,2,1,0:T(8,128)} custom-call(bf16[1,128,8192]{2,1,0:T(8,128)(2,1)} %dec_hbm.1, bf16[1,8192,768]{2,1,0:T(8,128)(2,1)} %enc_hbm.1, bf16[256,1024]{1,0:T(8,128)(2,1)} %act_hbm.1, bf16[256,6144]{1,0:T(8,128)(2,1)} %grad_hbm.1, s32[1,1,24]{2,1,0:T(1,128)} %src_ref.1, s32[1,1,24]{2,1,0:T(1,128)} %tgt_ref.1), custom_call_target="tpu_custom_call" | custom-call | flops 8053063680 | bytes 18350080 | tf_op jit(solution)/shard_map/pallas_call | solution.py:259
  100.1 2.7 %broadcast_select_fusion = f32[1,1,24,128,128]{4,3,2,1,0:T(8,128)} fusion(f32[1,1,24,128,128]{4,3,2,1,0:T(8,128)} %shard_map.73, pred[24]{0:T(512)(128)(4,1)S(1)} %iota_compare_fusion), kind=kLoop, calls=%fused_computation | loop fusion | flops 393216 | bytes 3145752 | tf_op jit(solution)/shard_map/jit(_where)/select_n | solution.py:292
  (1 shorter events, 0.0 us)

commit v2 on v1

--- a/solution.py
+++ b/solution.py
@@ -212,13 +212,9 @@
 
     grad_own.wait()
     correlate(me_f)
-    for i in arrivals[:4]:
+    for i in arrivals:
         receive_grad(i)
-    for key in last[:2]:
-        receive(*key)
-    for i in arrivals[4:]:
-        receive_grad(i)
-    for key in last[2:]:
+    for key in last:
         receive(*key)
 
     for j in range(layers):

time: 103 us -> 102 us (level)
  Pallas kernels: 99.4 us -> 98.2 us
    pallas_call x1, Pallas kernels: 99.4 us -> 98.2 us  [local(): pl.pallas_call(functools.partial(kernel, layers, feats), out_shape=jax.Sh...]
where the time goes in v2:
time: 102 us
  Pallas kernels  98.2 us (96%)
  other arithmetic  2.73 us (3%)
    pallas_call x1, Pallas kernels, local(): pl.pallas_call(functools.partial(kernel, layers, feats), out_shape=jax.Sh...  98.2 us
    select_n x1, other arithmetic, local(): return jnp.where(live, edges, 0.0)  2.72 us

profile of v2, /device:TPU:0, one launch (start us, length us, event | category | flops | bytes accessed | tf_op | source)
XLA Modules:
  0.0 101.6 jit_solution(2738770013426467257)
XLA Ops:
  0.7 98.2 %shard_map.73 = f32[1,1,24,128,128]{4,3,2,1,0:T(8,128)} custom-call(bf16[1,128,8192]{2,1,0:T(8,128)(2,1)} %dec_hbm.1, bf16[1,8192,768]{2,1,0:T(8,128)(2,1)} %enc_hbm.1, bf16[256,1024]{1,0:T(8,128)(2,1)} %act_hbm.1, bf16[256,6144]{1,0:T(8,128)(2,1)} %grad_hbm.1, s32[1,1,24]{2,1,0:T(1,128)} %src_ref.1, s32[1,1,24]{2,1,0:T(1,128)} %tgt_ref.1), custom_call_target="tpu_custom_call" | custom-call | flops 8053063680 | bytes 18350080 | tf_op jit(solution)/shard_map/pallas_call | solution.py:255
  98.9 2.7 %broadcast_select_fusion = f32[1,1,24,128,128]{4,3,2,1,0:T(8,128)} fusion(f32[1,1,24,128,128]{4,3,2,1,0:T(8,128)} %shard_map.73, pred[24]{0:T(512)(128)(4,1)S(1)} %iota_compare_fusion), kind=kLoop, calls=%fused_computation | loop fusion | flops 393216 | bytes 3145752 | tf_op jit(solution)/shard_map/jit(_where)/select_n | solution.py:288
  (1 shorter events, 0.0 us)
